TPU v7x, 256 devices: a whole 4x4x8 slice. The times are simulated.
256 devices in a mesh: seq: 64 (over x, z, core), chan: 4 (over y).
Axes of the slice: x: 4, y: 4, z: 8, core: 2. Of those that a mesh axis runs over, the one named last changes fastest.
Arguments:
- query_proj: bfloat16 [16384, 4096], P('seq', 'chan'), may hold values from -6 to 6
- key_proj: bfloat16 [16384, 4096], P('seq', 'chan'), may hold values from -6 to 6
- value_proj: bfloat16 [16384, 4096], P('seq', 'chan'), may hold values from -6 to 6
- residues: float32 [4096, 16], P('chan'), may hold values from -0.09375 to 0.09375
- pole_rates: float32 [4096, 16], P('chan'), may hold values from 0.5 to 1000
- skip_gain: float32 [4096], P('chan'), may hold values from 0.25 to 1
- norm_gain: float32 [4096], P('chan'), may hold values from 0.1 to 1.9
Outputs:
- normed: bfloat16 [16384, 4096], P('seq', 'chan')
All inputs are finite; a program needn't handle non-finite values.
Results may differ from a plain program's by a relative error of at most 0.001.
Values sent between devices are 32-bit elements; how exact they have to be, the bound alone decides.
A program may use at most 128 MiB of HBM per device.

v0:
```python
import math

import jax
import jax.numpy as jnp
from jax import lax
from jax.sharding import PartitionSpec as P

highest = lax.Precision.HIGHEST


def dft_table(size, sign):
    index = jnp.arange(size, dtype=jnp.int32)
    angle = (index[:, None] * index[None, :] % size).astype(jnp.float32) * (2.0 * math.pi / size)
    return (jnp.cos(angle), sign * jnp.sin(angle))


def apply_table(table, blocks, form):
    cosines, sines = table

    def product(left, right):
        return jnp.einsum(form, left, right, precision=highest)

    return jnp.stack(
        [
            product(cosines, blocks[0]) - product(sines, blocks[1]),
            product(cosines, blocks[1]) + product(sines, blocks[0]),
        ]
    )


def rotate(blocks, angle):
    cosines = jnp.cos(angle)
    sines = jnp.sin(angle)
    return jnp.stack(
        [blocks[0] * cosines - blocks[1] * sines, blocks[0] * sines + blocks[1] * cosines]
    )


def forward(signal, position, devices, first_step, second_step):
    tok_count = signal.shape[0]
    length = tok_count * devices
    group = tok_count // devices
    pieces = first_step(signal[None])
    outer = jnp.arange(devices, dtype=jnp.int32)
    inner = position * group + jnp.arange(group, dtype=jnp.int32)
    spots = (outer[:, None] * tok_count + inner[None, :]).astype(jnp.float32)
    phase = spots * (math.pi / length)
    real_part = jnp.stack([pieces, pieces * jnp.cos(phase)[:, :, None]])
    imag_part = jnp.stack([jnp.zeros_like(pieces), -pieces * jnp.sin(phase)[:, :, None]])
    blocks = jnp.stack([real_part, imag_part])
    blocks = apply_table(dft_table(devices, -1.0), blocks, "ka,uabc->ukbc")
    angle = (outer[:, None] * inner[None, :] % length).astype(jnp.float32) * (
        -2.0 * math.pi / length
    )
    blocks = rotate(blocks, angle[:, :, None])
    blocks = second_step(blocks)
    return apply_table(dft_table(tok_count, -1.0), blocks, "kb,uabc->uakc")


def inverse(blocks, position, devices, first_step, second_step):
    tok_count = blocks.shape[3]
    length = tok_count * devices
    group = tok_count // devices
    blocks = apply_table(dft_table(tok_count, 1.0), blocks, "kb,uabc->uakc")
    inner = jnp.arange(tok_count, dtype=jnp.int32)
    angle = (position * inner % length).astype(jnp.float32) * (2.0 * math.pi / length)
    blocks = rotate(blocks, angle[None, :, None])
    blocks = first_step(blocks)
    blocks = apply_table(dft_table(devices, 1.0), blocks, "ka,uabc->ukbc")
    outer = jnp.arange(devices, dtype=jnp.int32)
    inner_rows = position * group + jnp.arange(group, dtype=jnp.int32)
    spots = (outer[:, None] * tok_count + inner_rows[None, :]).astype(jnp.float32)
    phase = spots * (math.pi / length)
    values = (
        blocks[0, 0]
        + blocks[0, 1] * jnp.cos(phase)[:, :, None]
        - blocks[1, 1] * jnp.sin(phase)[:, :, None]
    ) / (2.0 * length)
    return second_step(values)[0]


def mode_column(table, mode):
    return lax.dynamic_slice_in_dim(table, mode, 1, 1)[:, 0]


def modal_table(residues, pole_rates, positions, length):

    def add_mode(mode, total):
        rate = mode_column(pole_rates, mode)
        weight = mode_column(residues, mode)
        return total + weight[:, None] * jnp.exp(-rate[:, None] * positions[None, :] / length)

    empty = jnp.zeros((residues.shape[0], positions.shape[0]), jnp.float32)
    return lax.fori_loop(0, residues.shape[1], add_mode, empty)


def complex_product(left, right):
    return jnp.stack(
        [left[0] * right[0] - left[1] * right[1], left[0] * right[1] + left[1] * right[0]]
    )


def by_spectrum(gated, residues, pole_rates, position, devices, tok_count):
    length = tok_count * devices
    start = position * tok_count

    def signal_out(blocks):
        return lax.all_to_all(blocks, "seq", split_axis=1, concat_axis=0, tiled=True)

    def signal_back(blocks):
        return lax.all_to_all(blocks, "seq", split_axis=2, concat_axis=3, tiled=True)

    signal_spec = forward(gated, position, devices, signal_out, signal_back)

    def filter_out(blocks):
        return lax.all_to_all(blocks, "seq", split_axis=1, concat_axis=0, tiled=True)

    def filter_back(blocks):
        return lax.all_to_all(blocks, "seq", split_axis=2, concat_axis=3, tiled=True)

    positions = (start + jnp.arange(tok_count, dtype=jnp.int32)).astype(jnp.float32)
    kernel = modal_table(residues, pole_rates, positions, length).T
    filter_spec = forward(kernel, position, devices, filter_out, filter_back)
    product = complex_product(signal_spec, filter_spec)

    def spectrum_out(blocks):
        return lax.all_to_all(blocks, "seq", split_axis=3, concat_axis=2, tiled=True)

    def spectrum_back(values):
        return lax.all_to_all(values, "seq", split_axis=0, concat_axis=1, tiled=True)

    return inverse(product, position, devices, spectrum_out, spectrum_back)


def per_device(query_proj, key_proj, value_proj, residues, pole_rates, skip_gain, norm_gain):
    tok_count = query_proj.shape[0]
    devices = lax.axis_size("seq")
    position = lax.axis_index("seq")
    gated = key_proj.astype(jnp.float32) * value_proj.astype(jnp.float32)
    convolved = by_spectrum(gated, residues, pole_rates, position, devices, tok_count)
    mixture = query_proj.astype(jnp.float32) * (convolved + skip_gain[None, :] * gated)
    squares = lax.psum(jnp.sum(mixture * mixture, axis=1), "chan")
    channels = mixture.shape[1] * lax.axis_size("chan")
    scale = lax.rsqrt(squares / channels + 1e-06)
    return (mixture * scale[:, None] * norm_gain[None, :]).astype(jnp.bfloat16)


def solution(mesh):
    return jax.shard_map(
        per_device,
        mesh=mesh,
        in_specs=(
            P("seq", "chan"),
            P("seq", "chan"),
            P("seq", "chan"),
            P("chan", None),
            P("chan", None),
            P("chan"),
            P("chan"),
        ),
        out_specs=P("seq", "chan"),
        check_vma=False,
    )
```

profile of v0, /device:TPU:6, one launch (start us, length us, event | category | flops | bytes accessed | tf_op | source)
XLA Modules:
  0.0 550.9 jit_solution(15532845217607724369)
XLA Ops:
  0.0 24.9 %while.14 = (s32[]{:T(128)}, f32[1024,256]{1,0:T(8,128)S(1)}, f32[1024,16]{0,1:T(8,128)}, f32[1024,16]{0,1:T(8,128)}, s32[]{:T(128)}, /*index=5*/s32[]{:T(128)}, s32[]{:T(128)}) while((s32[]{:T(128)}, f32[1024,256]{1,0:T(8,128)S(1)}, f32[1024,16]{0,1:T(8,128)}, f32[1024,16]{0,1:T(8,128)}, s32[]{:T(128)}, /*index=5*/s32[]{:T(128)}, ...), condition=%wide.region_1.2_spmd.clone, body=%wide.region_0.1_spmd.clone.sunk | while | flops 1312259 | bytes 2123879 | solution.py:94
  27.0 12.2 %all-to-all-start.2 = ((f32[1,256,1024]{2,0,1:T(1,128)}), f32[1,256,1024]{2,0,1:T(1,128)S(1)}, u32[]{:S(2)}, u32[]{:S(2)}) async-start(f32[1,256,1024]{2,0,1:T(1,128)} %broadcast_in_dim.10), calls=%async_computation.2 | async-start | bytes 2097152 | tf_op jit(solution)/shard_map/all_to_all | solution.py:116
  41.4 24.4 %all-to-all-done.2 = f32[1,256,1024]{2,0,1:T(1,128)S(1)} async-done(((f32[1,256,1024]{2,0,1:T(1,128)}), f32[1,256,1024]{2,0,1:T(1,128)S(1)}, u32[]{:S(2)}, u32[]{:S(2)}) %all-to-all-start.2) | async-done | bytes 1048608 | tf_op jit(solution)/shard_map/all_to_all | solution.py:116
  65.8 8.4 %all-to-all-start = ((f32[1,256,1024]{2,0,1:T(1,128)}), f32[1,256,1024]{2,0,1:T(1,128)S(1)}, u32[]{:S(2)}, u32[]{:S(2)}) async-start(f32[1,256,1024]{2,0,1:T(1,128)} %copy.38), calls=%async_computation | async-start | bytes 2097152 | tf_op jit(solution)/shard_map/all_to_all | solution.py:108
  74.3 3.5 fusion.57
  77.9 3.5 fusion.56
  81.4 19.2 %all-to-all-done = f32[1,256,1024]{2,0,1:T(1,128)S(1)} async-done(((f32[1,256,1024]{2,0,1:T(1,128)}), f32[1,256,1024]{2,0,1:T(1,128)S(1)}, u32[]{:S(2)}, u32[]{:S(2)}) %all-to-all-start) | async-done | bytes 1048608 | tf_op jit(solution)/shard_map/all_to_all | solution.py:108
  114.1 4.5 fusion.15
  119.1 4.6 copy.51
  123.8 8.6 %all-to-all-start.3 = ((f32[2,2,64,4,1024]{4,3,1,0,2:T(4,128)}), f32[2,2,64,4,1024]{4,3,1,0,2:T(4,128)}, u32[]{:S(2)}, u32[]{:S(2)}) async-start(f32[2,2,64,4,1024]{4,3,1,0,2:T(4,128)} %copy.51), calls=%async_computation.3 | async-start | bytes 8388608 | tf_op jit(solution)/shard_map/all_to_all | solution.py:119
  134.3 4.7 copy.42
  139.1 87.1 %all-to-all-done.3 = f32[2,2,64,4,1024]{4,3,1,0,2:T(4,128)} async-done(((f32[2,2,64,4,1024]{4,3,1,0,2:T(4,128)}), f32[2,2,64,4,1024]{4,3,1,0,2:T(4,128)}, u32[]{:S(2)}, u32[]{:S(2)}) %all-to-all-start.3) | async-done | bytes 4194336 | tf_op jit(solution)/shard_map/all_to_all | solution.py:119
  226.1 7.9 %all-to-all-start.1 = ((f32[2,2,64,4,1024]{4,3,1,0,2:T(4,128)}), f32[2,2,64,4,1024]{4,3,1,0,2:T(4,128)}, u32[]{:S(2)}, u32[]{:S(2)}) async-start(f32[2,2,64,4,1024]{4,3,1,0,2:T(4,128)} %copy.42), calls=%async_computation.1 | async-start | bytes 8388608 | tf_op jit(solution)/shard_map/all_to_all | solution.py:111
  234.1 4.9 fusion.271
  239.0 3.3 copy.52
  245.1 4.9 copy.54
  250.0 4.3 copy.55
  260.0 4.2 convolution_subtract_fusion
  264.2 4.2 convolution_add_fusion
  268.4 59.5 %all-to-all-done.1 = f32[2,2,64,4,1024]{4,3,1,0,2:T(4,128)} async-done(((f32[2,2,64,4,1024]{4,3,1,0,2:T(4,128)}), f32[2,2,64,4,1024]{4,3,1,0,2:T(4,128)}, u32[]{:S(2)}, u32[]{:S(2)}) %all-to-all-start.1) | async-done | bytes 4194336 | tf_op jit(solution)/shard_map/all_to_all | solution.py:111
  327.9 5.4 fusion.272
  339.3 4.1 fusion.79
  346.6 4.3 copy.46
  350.9 4.5 fusion.75
  375.6 7.4 %copy.60 = f32[2,2,1,256,1024]{4,1,2,0,3:T(2,128)} copy(f32[2,2,1,256,1024]{3,4,1,2,0:T(8,128)} %pad_maximum_fusion.2) | data formatting | bytes 8388608 | tf_op jit(solution)/shard_map/stack | solution.py:34
  383.0 101.7 %all_to_all.60 = f32[2,2,1,256,1024]{4,1,2,0,3:T(2,128)S(1)} all-to-all(f32[2,2,1,256,1024]{4,1,2,0,3:T(2,128)} %copy.60), channel_id=1, replica_groups=mesh['seq'=64,'chan'=4] {'seq'}, dimensions={3} | all-to-all | bytes 8388608 | tf_op jit(solution)/shard_map/all_to_all | solution.py:127
  486.2 3.6 fusion.22
  489.9 3.6 fusion.24
  493.5 4.0 subtract_bitcast_fusion
  497.6 3.8 add_bitcast_fusion
  502.4 34.6 %all_to_all.61 = f32[64,4,1024]{2,1,0:T(4,128)S(1)} all-to-all(f32[64,4,1024]{2,1,0:T(4,128)S(1)} %copy.65), channel_id=1, replica_groups=mesh['seq'=64,'chan'=4] {'seq'}, dimensions={0} | all-to-all | bytes 2097152 | tf_op jit(solution)/shard_map/all_to_all | solution.py:130
  538.8 10.7 %psum.7 = f32[256]{0:T(256)S(1)} all-reduce(f32[256]{0:T(256)S(1)} %multiply_reduce_fusion), channel_id=1, replica_groups=mesh['seq'=64,'chan'=4] {'chan'}, use_global_device_ids=true, to_apply=%region_3.4 | all-reduce | flops 256 | bytes 2048 | tf_op jit(solution)/shard_map/psum | solution.py:142
  (111 shorter events, 87.9 us)
Async XLA Ops:
  25.2 13.9 %copy-start.8 = (bf16[256,1024]{1,0:T(8,128)(2,1)S(1)}, bf16[256,1024]{1,0:T(8,128)(2,1)}, u32[]{:S(2)}) copy-start(bf16[256,1024]{1,0:T(8,128)(2,1)} %param.11) | copy-start | bytes 1572868
  25.2 13.9 %copy-start.9 = (bf16[256,1024]{1,0:T(8,128)(2,1)S(1)}, bf16[256,1024]{1,0:T(8,128)(2,1)}, u32[]{:S(2)}) copy-start(bf16[256,1024]{1,0:T(8,128)(2,1)} %param.10) | copy-start | bytes 1572868
  27.0 38.8 %all-to-all-start.2 = ((f32[1,256,1024]{2,0,1:T(1,128)}), f32[1,256,1024]{2,0,1:T(1,128)S(1)}, u32[]{:S(2)}, u32[]{:S(2)}) async-start(f32[1,256,1024]{2,0,1:T(1,128)} %broadcast_in_dim.10), calls=%async_computation.2 | async-start | bytes 2097152 | tf_op jit(solution)/shard_map/all_to_all | solution.py:116
  65.8 34.8 %all-to-all-start = ((f32[1,256,1024]{2,0,1:T(1,128)}), f32[1,256,1024]{2,0,1:T(1,128)S(1)}, u32[]{:S(2)}, u32[]{:S(2)}) async-start(f32[1,256,1024]{2,0,1:T(1,128)} %copy.38), calls=%async_computation | async-start | bytes 2097152 | tf_op jit(solution)/shard_map/all_to_all | solution.py:108
  109.2 2.5 copy-start.5
  111.7 2.4 copy-start.4
  123.8 102.3 %all-to-all-start.3 = ((f32[2,2,64,4,1024]{4,3,1,0,2:T(4,128)}), f32[2,2,64,4,1024]{4,3,1,0,2:T(4,128)}, u32[]{:S(2)}, u32[]{:S(2)}) async-start(f32[2,2,64,4,1024]{4,3,1,0,2:T(4,128)} %copy.51), calls=%async_computation.3 | async-start | bytes 8388608 | tf_op jit(solution)/shard_map/all_to_all | solution.py:119
  226.1 101.8 %all-to-all-start.1 = ((f32[2,2,64,4,1024]{4,3,1,0,2:T(4,128)}), f32[2,2,64,4,1024]{4,3,1,0,2:T(4,128)}, u32[]{:S(2)}, u32[]{:S(2)}) async-start(f32[2,2,64,4,1024]{4,3,1,0,2:T(4,128)} %copy.42), calls=%async_computation.1 | async-start | bytes 8388608 | tf_op jit(solution)/shard_map/all_to_all | solution.py:111
  254.3 2.9 copy-start
  339.3 4.1 copy-start.7
  350.9 4.5 copy-start.1
  350.9 4.5 copy-start.6
  355.5 2.9 copy-start.2
  355.5 2.9 copy-start.3
  502.4 34.9 %copy-start.11 = (f32[1024]{0:T(1024)S(1)}, f32[1024]{0:T(1024)}, u32[]{:S(2)}) copy-start(f32[1024]{0:T(1024)} %param.14) | copy-start | bytes 12292
  536.9 12.6 %copy-start.12 = (f32[1024]{0:T(1024)S(1)}, f32[1024]{0:T(1024)}, u32[]{:S(2)}) copy-start(f32[1024]{0:T(1024)} %param.15) | copy-start | bytes 12292
  537.3 12.2 %copy-start.10 = (bf16[256,1024]{1,0:T(8,128)(2,1)S(1)}, bf16[256,1024]{1,0:T(8,128)(2,1)}, u32[]{:S(2)}) copy-start(bf16[256,1024]{1,0:T(8,128)(2,1)} %param.9) | copy-start | bytes 1572868
where the time goes:
time: 558 us; the launch traced here: 551 us
  waiting for transfers between devices  190 us (34%)
  blocking collectives  147 us (26%)
  matrix products  79.4 us (14%)
  local copies, waits for them, and re-layouts  62.6 us (11%)
  starting transfers between devices  37.1 us (7%)
  other arithmetic  33.5 us (6%)
    all_to_all x1, blocking collectives, spectrum_out(): lax.all_to_all(blocks, 'seq', split_axis=3, concat_axis=2, tiled=True)  102 us
    all_to_all x1, waiting for transfers between devices, filter_back(): lax.all_to_all(blocks, 'seq', split_axis=2, concat_axis=3, tiled=True)  87.1 us
    dot_general x24, matrix products, product(): return jnp.einsum(form, left, right, precision=highest)  79.4 us
    all_to_all x1, waiting for transfers between devices, signal_back(): lax.all_to_all(blocks, 'seq', split_axis=2, concat_axis=3, tiled=True)  59.5 us
    all_to_all x1, blocking collectives, spectrum_back(): lax.all_to_all(values, 'seq', split_axis=0, concat_axis=1, tiled=True)  34.6 us
    all_to_all x1, waiting for transfers between devices, filter_out(): lax.all_to_all(blocks, 'seq', split_axis=1, concat_axis=0, tiled=True)  24.4 us
    all_to_all x1, waiting for transfers between devices, signal_out(): lax.all_to_all(blocks, 'seq', split_axis=1, concat_axis=0, tiled=True)  19.2 us
    slice x5, local copies, waits for them, and re-layouts, apply_table(): blocks[0]  18.4 us
  transfers between devices with their start and end apart: 4, of which 4 were waited for; matrix products, arithmetic and copies ran while one was open for 9% of the time, Pallas kernels for 0%

commit v1 on v0

v1 whole, which is shorter than its diff:
```python
import functools

import jax
import jax.numpy as jnp
from jax import lax
from jax.experimental import pallas as pl
from jax.experimental.pallas import tpu as pltpu
from jax.sharding import PartitionSpec as P

MESH = pl.DeviceIdType.MESH
F32 = jnp.float32
LANES = 128
SUB = 8
OWNER_Z = (0, 7)


def shift_rows(x, n, rows):
    return jnp.where(rows >= n, pltpu.roll(x, n, 0), 0.0)


def body(
    length,
    q_hbm,
    k_hbm,
    v_hbm,
    res_hbm,
    rate_hbm,
    skip_hbm,
    gain_hbm,
    out_ref,
    q_ref,
    k_ref,
    v_ref,
    res_ref,
    rate_ref,
    skip_ref,
    gain_ref,
    g_ref,
    y_ref,
    q32_ref,
    ends_ref,
    local_ref,
    state_ref,
    lead_ref,
    square_ref,
    scale_ref,
    pieces_ref,
    prefix_ref,
    part_ref,
    parts_ref,
    load_sem,
    send_sem,
    piece_sem,
    back_sem,
    state_sem,
    part_send,
    part_sem,
):
    me = lax.axis_index("seq")
    chan = lax.axis_index("chan")
    tokens, channels = q_ref.shape
    modes = res_ref.shape[0]
    tiles = channels // LANES
    steps = tokens // SUB
    devices = pieces_ref.shape[0]
    chans = parts_ref.shape[0] + 1
    groups = devices // SUB
    x, z, core = me // 16, lax.rem(me // 2, 8), lax.rem(me, 2)
    is_owner = (z == OWNER_Z[0]) | (z == OWNER_Z[1])
    high = jnp.where(z == OWNER_Z[1], 1, 0)
    owned = core + 2 * x + 8 * high

    def owner_of(half, tile):
        return ((tile // 2) * 8 + OWNER_Z[half]) * 2 + lax.rem(tile, 2)

    loads = [
        pltpu.make_async_copy(src, dst, load_sem.at[n])
        for n, (src, dst) in enumerate(
            (
                (k_hbm, k_ref),
                (v_hbm, v_ref),
                (rate_hbm, rate_ref),
                (res_hbm, res_ref),
                (q_hbm, q_ref),
                (skip_hbm, skip_ref),
                (gain_hbm, gain_ref),
            )
        )
    ]
    for load in loads:
        load.start()

    barrier = pltpu.get_barrier_semaphore()

    @pl.when(is_owner)
    def _():
        def greet(n, carry):
            pl.semaphore_signal(
                barrier, inc=1, device_id={"seq": lax.rem(me + n, devices)}, device_id_type=MESH
            )
            return carry

        lax.fori_loop(1, devices, greet, 0)

    for n in range(1, chans):
        pl.semaphore_signal(
            barrier, inc=1, device_id={"chan": lax.rem(chan + n, chans)}, device_id_type=MESH
        )

    rows = lax.broadcasted_iota(jnp.int32, (SUB, LANES), 0)
    rows_f = rows.astype(F32)
    sub = tokens // SUB

    for load in loads[:3]:
        load.wait()

    def row(ref, m, cols):
        return jnp.broadcast_to(ref[m : m + 1, cols], (SUB, LANES))

    def block_ends(tile, carry):
        cols = pl.ds(pl.multiple_of(tile * LANES, LANES), LANES)
        g_ref[tile] = k_ref[:, cols].astype(F32) * v_ref[:, cols].astype(F32)
        rates = [row(rate_ref, m, cols) * (-1.0 / length) for m in range(modes)]
        decay = [jnp.exp(r) for r in rates]
        held = None
        for i in range(sub):
            g = g_ref[tile, pl.ds(i, SUB, stride=sub), :]
            held = [g] * modes if held is None else [h * a + g for h, a in zip(held, decay)]
        for m in range(modes):
            ends_ref[tile, m] = held[m]
            weight = jnp.exp(rates[m] * (sub * (SUB - 1.0 - rows_f)))
            local_ref[m : m + 1, cols] = jnp.sum(held[m] * weight, axis=0, keepdims=True)
        return carry

    lax.fori_loop(0, tiles, block_ends, 0)

    pl.semaphore_wait(barrier, chans - 1 + jnp.where(is_owner, 2 * tiles - 1, 2 * tiles))

    def send_pieces(tile, carry):
        cols = pl.ds(pl.multiple_of(tile * LANES, LANES), LANES)
        for half in range(2):
            piece = local_ref.at[half * SUB : (half + 1) * SUB, cols]
            owner = owner_of(half, tile)

            @pl.when(owner == me)
            def _():
                pltpu.make_async_copy(piece, pieces_ref.at[me], piece_sem.at[me // SUB]).start()

            @pl.when(owner != me)
            def _():
                pltpu.make_async_remote_copy(
                    src_ref=piece,
                    dst_ref=pieces_ref.at[me],
                    send_sem=send_sem,
                    recv_sem=piece_sem.at[me // SUB],
                    device_id={"seq": owner},
                    device_id_type=MESH,
                ).start()

        return carry

    lax.fori_loop(0, tiles, send_pieces, 0)

    for load in loads[3:]:
        load.wait()

    def local_part(tile, carry):
        cols = pl.ds(pl.multiple_of(tile * LANES, LANES), LANES)
        q32_ref[tile] = q_ref[:, cols].astype(F32)
        decay, weight, held = [], [], []
        for m in range(modes):
            rate = row(rate_ref, m, cols) * (-1.0 / length)
            weight.append(row(res_ref, m, cols))
            decay.append(jnp.exp(rate))
            lead_ref[tile, m] = weight[m] * jnp.exp(rate * (rows_f + 1.0))
            long = jnp.exp(rate * sub)
            ends = ends_ref[tile, m]
            ends = ends + long * shift_rows(ends, 1, rows)
            long = long * long
            ends = ends + long * shift_rows(ends, 2, rows)
            long = long * long
            ends = ends + long * shift_rows(ends, 4, rows)
            held.append(shift_rows(ends, 1, rows))
        skip = row(skip_ref, 0, cols)
        for i in range(sub):
            spots = pl.ds(i, SUB, stride=sub)
            g = g_ref[tile, spots, :]
            held = [h * a + g for h, a in zip(held, decay)]
            terms = [h * w for h, w in zip(held, weight)] + [skip * g]
            while len(terms) > 1:
                terms = [sum(terms[n : n + 2]) for n in range(0, len(terms), 2)]
            y_ref[tile, spots, :] = terms[0]
        return carry

    lax.fori_loop(0, tiles, local_part, 0)
    square_ref[...] = jnp.zeros_like(square_ref)

    @pl.when(is_owner)
    def _():
        half_rows = pl.ds(pl.multiple_of(high * SUB, SUB), SUB)
        cols = pl.ds(pl.multiple_of((core + 2 * x) * LANES, LANES), LANES)
        whole = jnp.exp(rate_ref[half_rows, cols] * (-float(tokens) / length))
        prefix_ref[0] = jnp.zeros((SUB, LANES), F32)

        def send_back(to):
            @pl.when(to == me)
            def _():
                pltpu.make_async_copy(
                    prefix_ref.at[to], state_ref.at[half_rows, cols], state_sem
                ).start()

            @pl.when(to != me)
            def _():
                pltpu.make_async_remote_copy(
                    src_ref=prefix_ref.at[to],
                    dst_ref=state_ref.at[half_rows, cols],
                    send_sem=back_sem,
                    recv_sem=state_sem,
                    device_id={"seq": to},
                    device_id_type=MESH,
                ).start()

        def group(n, total):
            mine = pieces_ref.at[pl.ds(n * SUB, SUB)]
            pltpu.make_async_copy(mine, mine, piece_sem.at[n]).wait()

            def one(j, total):
                p = n * SUB + j
                prefix_ref[p] = total
                send_back(p)
                return total * whole + pieces_ref[p]

            return lax.fori_loop(0, SUB, one, total)

        lax.fori_loop(0, groups, group, jnp.zeros((SUB, LANES), F32))

    pltpu.make_async_copy(state_ref, state_ref, state_sem).wait()

    def add_state(tile, carry):
        cols = pl.ds(pl.multiple_of(tile * LANES, LANES), LANES)
        eighth = [jnp.exp(row(rate_ref, m, cols) * (-float(SUB) / length)) for m in range(modes)]
        terms = [lead_ref[tile, m] * row(state_ref, m, cols) for m in range(modes)]
        for i in range(steps):
            spots = pl.ds(i * SUB, SUB)
            total = list(terms)
            while len(total) > 1:
                total = [total[n] + total[n + 1] for n in range(0, len(total), 2)]
            mixed = q32_ref[tile, spots, :] * (y_ref[tile, spots, :] + total[0])
            y_ref[tile, spots, :] = mixed
            square_ref[spots, :] += mixed * mixed
            if i + 1 < steps:
                terms = [t * a for t, a in zip(terms, eighth)]
        return carry

    lax.fori_loop(0, tiles, add_state, 0)

    lanes = lax.broadcasted_iota(jnp.int32, (SUB, LANES), 1)
    part = jnp.zeros((SUB, LANES), F32)
    for i in range(steps):
        sums = jnp.sum(square_ref[i * SUB : (i + 1) * SUB, :], axis=1, keepdims=True)
        part = jnp.where(lanes == i, sums, part)
    part_ref[...] = part
    for n in range(1, chans):
        pltpu.make_async_remote_copy(
            src_ref=part_ref,
            dst_ref=parts_ref.at[n - 1],
            send_sem=part_send,
            recv_sem=part_sem,
            device_id={"chan": lax.rem(chan + n, chans)},
            device_id_type=MESH,
        ).start()
    pltpu.make_async_copy(parts_ref, parts_ref, part_sem).wait()
    whole_sum = part
    for n in range(1, chans):
        whole_sum = whole_sum + parts_ref[n - 1]
    scale = lax.rsqrt(whole_sum * (1.0 / (channels * chans)) + 1e-06)
    for i in range(steps):
        scale_ref[i * SUB : (i + 1) * SUB, :] = jnp.broadcast_to(scale[:, i : i + 1], (SUB, LANES))

    def finish(tile, carry):
        cols = pl.ds(pl.multiple_of(tile * LANES, LANES), LANES)
        out_ref[:, cols] = (y_ref[tile] * scale_ref[...] * gain_ref[:, cols]).astype(out_ref.dtype)
        return carry

    lax.fori_loop(0, tiles, finish, 0)

    pltpu.make_async_copy(parts_ref, parts_ref, part_send).wait()

    @pl.when(is_owner)
    def _():
        sent = pieces_ref.at[pl.ds(0, 2 * tiles - 1)]
        pltpu.make_async_copy(sent, sent, send_sem).wait()
        back = pieces_ref.at[pl.ds(0, devices - 1)]
        pltpu.make_async_copy(back, back, back_sem).wait()

    @pl.when(jnp.logical_not(is_owner))
    def _():
        sent = pieces_ref.at[pl.ds(0, 2 * tiles)]
        pltpu.make_async_copy(sent, sent, send_sem).wait()


def per_device(devices, chans, q, k, v, residues, rates, skip, gain):
    tokens, channels = q.shape
    modes = residues.shape[1]
    tiles = channels // LANES
    bf16 = q.dtype
    inputs = (q, k, v, residues.T, rates.T, skip[None, :], gain[None, :])
    vmem = pltpu.VMEM
    return pl.pallas_call(
        functools.partial(body, float(tokens * devices)),
        out_shape=jax.ShapeDtypeStruct((tokens, channels), bf16),
        in_specs=[pl.BlockSpec(memory_space=pltpu.HBM)] * len(inputs),
        out_specs=pl.BlockSpec(memory_space=vmem),
        scratch_shapes=[
            vmem((tokens, channels), bf16),
            vmem((tokens, channels), bf16),
            vmem((tokens, channels), bf16),
            vmem((modes, channels), F32),
            vmem((modes, channels), F32),
            vmem((1, channels), F32),
            vmem((1, channels), F32),
            vmem((tiles, tokens, LANES), F32),
            vmem((tiles, tokens, LANES), F32),
            vmem((tiles, tokens, LANES), F32),
            vmem((tiles, modes, SUB, LANES), F32),
            vmem((modes, channels), F32),
            vmem((modes, channels), F32),
            vmem((tiles, modes, SUB, LANES), F32),
            vmem((tokens, LANES), F32),
            vmem((tokens, LANES), F32),
            vmem((devices, SUB, LANES), F32),
            vmem((devices, SUB, LANES), F32),
            vmem((SUB, LANES), F32),
            vmem((chans - 1, SUB, LANES), F32),
            pltpu.SemaphoreType.DMA((7,)),
            pltpu.SemaphoreType.DMA,
            pltpu.SemaphoreType.DMA((devices // SUB,)),
            pltpu.SemaphoreType.DMA,
            pltpu.SemaphoreType.DMA,
            pltpu.SemaphoreType.DMA,
            pltpu.SemaphoreType.DMA,
        ],
        compiler_params=pltpu.CompilerParams(
            collective_id=0, has_side_effects=True, vmem_limit_bytes=24 * 1024 * 1024
        ),
    )(*[pltpu.with_memory_space_constraint(a, pltpu.HBM) for a in inputs])


def solution(mesh):
    devices, chans = mesh.shape["seq"], mesh.shape["chan"]
    return jax.shard_map(
        functools.partial(per_device, devices, chans),
        mesh=mesh,
        in_specs=(
            P("seq", "chan"),
            P("seq", "chan"),
            P("seq", "chan"),
            P("chan", None),
            P("chan", None),
            P("chan"),
            P("chan"),
        ),
        out_specs=P("seq", "chan"),
        check_vma=False,
    )
```

time: 558 us -> 29.7 us (0.05)
  the two profiles are of different devices: /device:TPU:6 before, /device:TPU:1 now
where the time goes in v1:
time: 29.7 us; the launch traced here: 29.6 us
  Pallas kernels  28.8 us (97%)
  local copies, waits for them, and re-layouts  0.8 us (3%)
    pallas_call x1, Pallas kernels, per_device(): pl.pallas_call(functools.partial(body, float(tokens * devices)), out_shap...  28.8 us
    unnamed x1, local copies, waits for them, and re-layouts  0.8 us

profile of v1, /device:TPU:1, one launch (start us, length us, event | category | flops | bytes accessed | tf_op | source)
XLA Modules:
  0.0 29.6 jit_solution(6397959068603542415)
XLA Ops:
  0.0 28.8 %shard_map.73 = bf16[256,1024]{1,0:T(8,128)(2,1)S(1)} custom-call(bf16[256,1024]{1,0:T(8,128)(2,1)} %q_hbm.1, bf16[256,1024]{1,0:T(8,128)(2,1)} %k_hbm.1, bf16[256,1024]{1,0:T(8,128)(2,1)} %v_hbm.1, f32[16,1024]{1,0:T(8,128)} %bitcast.4, f32[16,1024]{1,0:T(8,128)} %bitcast.5, f32[1,1024]{1,0:T(1,128)} %bitcast.6, f32[1,1024]{1,0:T(1,128)} %bitcast.7), custom_call_target="tpu_custom_call" | custom-call | tf_op jit(solution)/shard_map/pallas_call | solution.py:309
  28.8 0.8 %copy.9 = bf16[256,1024]{1,0:T(8,128)(2,1)} copy(bf16[256,1024]{1,0:T(8,128)(2,1)S(1)} %shard_map.73) | data formatting | bytes 1048576

commit v2 on v1

v2 whole, which is shorter than its diff:
```python
import functools

import jax
import jax.numpy as jnp
from jax import lax
from jax.experimental import pallas as pl
from jax.experimental.pallas import tpu as pltpu
from jax.sharding import PartitionSpec as P

MESH = pl.DeviceIdType.MESH
F32 = jnp.float32
LANES = 128
SUB = 8
OWNER_Z = (0, 1)


def shift_rows(x, n, rows):
    return jnp.where(rows >= n, pltpu.roll(x, n, 0), 0.0)


def body(
    length,
    q_hbm,
    k_hbm,
    v_hbm,
    res_hbm,
    rate_hbm,
    skip_hbm,
    gain_hbm,
    out_ref,
    q_ref,
    k_ref,
    v_ref,
    res_ref,
    rate_ref,
    skip_ref,
    gain_ref,
    decay_ref,
    g_ref,
    y_ref,
    q32_ref,
    ends_ref,
    lead_ref,
    local_ref,
    other_ref,
    chip_ref,
    state_ref,
    start_ref,
    square_ref,
    scale_ref,
    pieces_ref,
    prefix_ref,
    part_ref,
    parts_ref,
    load_sem,
    key_sem,
    value_sem,
    other_sem,
    send_sem,
    piece_sem,
    back_sem,
    state_sem,
    part_send,
    part_sem,
):
    me = lax.axis_index("seq")
    chan = lax.axis_index("chan")
    tokens, channels = q_ref.shape
    modes = res_ref.shape[0]
    tiles = channels // LANES
    steps = tokens // SUB
    sub = tokens // SUB
    chips = pieces_ref.shape[0]
    devices = 2 * chips
    chans = parts_ref.shape[0] + 1
    chip = me // 2
    x, z, core = me // 16, lax.rem(chip, 8), lax.rem(me, 2)
    is_owner = z == OWNER_Z[0]
    which = 0
    for n in range(1, len(OWNER_Z)):
        is_owner = is_owner | (z == OWNER_Z[n])
        which = jnp.where(z == OWNER_Z[n], n, which)
    depth = modes // len(OWNER_Z)
    pieces = len(OWNER_Z) * tiles
    own_tile = core + 2 * x

    def owner_of(n, tile):
        return ((tile // 2) * 8 + OWNER_Z[n]) * 2 + lax.rem(tile, 2)

    def far_first(n):
        pair = n // 2
        turn = jnp.where(pair == 0, 2, jnp.where(pair == 1, 1, jnp.where(pair == 2, 3, 0)))
        return lax.rem(x + turn, 4) * 2 + lax.rem(n, 2)

    def near_first(n):
        pair = n // 2
        turn = jnp.where(pair == 2, 3, jnp.where(pair == 3, 2, pair))
        return lax.rem(x + turn, 4) * 2 + lax.rem(n, 2)

    def lanes_of(tile, width=1):
        return pl.ds(pl.multiple_of(tile * LANES, LANES), width * LANES)

    def load(src, dst, sem):
        return pltpu.make_async_copy(src, dst, sem)

    rate_load = load(rate_hbm, rate_ref, load_sem.at[0])
    rate_load.start()

    def load_pair(pair):
        cols = lanes_of(far_first(2 * pair), 2)
        return (
            load(k_hbm.at[:, cols], k_ref.at[:, cols], key_sem.at[pair]),
            load(v_hbm.at[:, cols], v_ref.at[:, cols], value_sem.at[pair]),
        )

    for pair in range(tiles // 2):
        for copy in load_pair(pair):
            copy.start()
    late_loads = [
        load(src, dst, load_sem.at[n + 1])
        for n, (src, dst) in enumerate(
            ((res_hbm, res_ref), (q_hbm, q_ref), (skip_hbm, skip_ref), (gain_hbm, gain_ref))
        )
    ]
    for copy in late_loads:
        copy.start()

    barrier = pltpu.get_barrier_semaphore()

    @pl.when(is_owner)
    def _():
        def greet(n, carry):
            sender = lax.rem(chip + n, chips) * 2 + 1

            @pl.when(sender != me)
            def _():
                pl.semaphore_signal(
                    barrier, inc=1, device_id={"seq": sender}, device_id_type=MESH
                )

            return carry

        lax.fori_loop(0, chips, greet, 0)

    @pl.when(core == 1)
    def _():
        pl.semaphore_signal(barrier, inc=1, device_id={"seq": me - 1}, device_id_type=MESH)

    for n in range(1, chans):
        pl.semaphore_signal(
            barrier, inc=1, device_id={"chan": lax.rem(chan + n, chans)}, device_id_type=MESH
        )

    rows = lax.broadcasted_iota(jnp.int32, (SUB, LANES), 0)
    rows_f = rows.astype(F32)

    rate_load.wait()
    for n, power in enumerate((1, sub, 2 * sub, 4 * sub)):
        decay_ref[n] = jnp.exp(rate_ref[...] * (-float(power) / length))

    def row(ref, m, cols):
        return jnp.broadcast_to(ref[m : m + 1, cols], (SUB, LANES))

    greetings = jnp.where(core == 1, pieces - jnp.where(is_owner, 1, 0), 1)
    pl.semaphore_wait(barrier, chans - 1 + greetings)

    def block_ends(n, carry):
        tile = far_first(n)
        cols = lanes_of(tile)

        @pl.when(lax.rem(n, 2) == 0)
        def _():
            for copy in load_pair(n // 2):
                copy.wait()

        g_ref[tile] = k_ref[:, cols].astype(F32) * v_ref[:, cols].astype(F32)
        decay = [row(decay_ref.at[0], m, cols) for m in range(modes)]
        held = None
        for i in range(sub):
            g = g_ref[tile, pl.ds(i, SUB, stride=sub), :]
            held = [g] * modes if held is None else [h * a + g for h, a in zip(held, decay)]
        for m in range(modes):
            end = held[m]
            ends_ref[tile, m] = end
            end = end + row(decay_ref.at[1], m, cols) * pltpu.roll(end, 1, 0)
            end = end + row(decay_ref.at[2], m, cols) * pltpu.roll(end, 2, 0)
            end = end + row(decay_ref.at[3], m, cols) * pltpu.roll(end, 4, 0)
            local_ref[m : m + 1, cols] = end[SUB - 1 :]

        @pl.when(core == 0)
        def _():
            pltpu.make_async_remote_copy(
                src_ref=local_ref.at[:, cols],
                dst_ref=other_ref.at[:, cols],
                send_sem=send_sem,
                recv_sem=other_sem.at[tile],
                device_id={"seq": me + 1},
                device_id_type=MESH,
            ).start()

        return carry

    lax.fori_loop(0, tiles, block_ends, 0)

    decay_ref[4] = jnp.exp(rate_ref[...] * (-float(tokens) / length))

    @pl.when(core == 1)
    def _():
        def send_pieces(n, carry):
            tile = far_first(n)
            cols = lanes_of(tile)
            mine = other_ref.at[:, cols]
            pltpu.make_async_copy(mine, mine, other_sem.at[tile]).wait()
            chip_ref[:, cols] = other_ref[:, cols] * decay_ref[4, :, cols] + local_ref[:, cols]
            for n in range(len(OWNER_Z)):
                piece = chip_ref.at[n * depth : (n + 1) * depth, cols]
                owner = owner_of(n, tile)

                @pl.when(owner == me)
                def _():
                    pltpu.make_async_copy(
                        piece, pieces_ref.at[chip], piece_sem.at[chip // 4]
                    ).start()

                @pl.when(owner != me)
                def _():
                    pltpu.make_async_remote_copy(
                        src_ref=piece,
                        dst_ref=pieces_ref.at[chip],
                        send_sem=send_sem,
                        recv_sem=piece_sem.at[chip // 4],
                        device_id={"seq": owner},
                        device_id_type=MESH,
                    ).start()

            return carry

        lax.fori_loop(0, tiles, send_pieces, 0)

    for copy in late_loads:
        copy.wait()
    decay_ref[5] = jnp.exp(rate_ref[...] * (-float(SUB) / length))

    @pl.when(core == 0)
    def _():
        other_ref[...] = jnp.zeros_like(other_ref)

    def local_part(tile, carry):
        cols = lanes_of(tile)
        q32_ref[tile] = q_ref[:, cols].astype(F32)
        decay, weight, held = [], [], []
        for m in range(modes):
            rate = row(rate_ref, m, cols) * (-1.0 / length)
            weight.append(row(res_ref, m, cols))
            decay.append(row(decay_ref.at[0], m, cols))
            lead_ref[tile, m] = weight[m] * jnp.exp(rate * (rows_f + 1.0))
            ends = ends_ref[tile, m]
            ends = ends + row(decay_ref.at[1], m, cols) * shift_rows(ends, 1, rows)
            ends = ends + row(decay_ref.at[2], m, cols) * shift_rows(ends, 2, rows)
            ends = ends + row(decay_ref.at[3], m, cols) * shift_rows(ends, 4, rows)
            held.append(shift_rows(ends, 1, rows))
        skip = row(skip_ref, 0, cols)
        for i in range(sub):
            spots = pl.ds(i, SUB, stride=sub)
            g = g_ref[tile, spots, :]
            held = [h * a + g for h, a in zip(held, decay)]
            terms = [h * w for h, w in zip(held, weight)] + [skip * g]
            while len(terms) > 1:
                terms = [sum(terms[n : n + 2]) for n in range(0, len(terms), 2)]
            y_ref[tile, spots, :] = terms[0]
        return carry

    lax.fori_loop(0, tiles, local_part, 0)
    square_ref[...] = jnp.zeros_like(square_ref)

    @pl.when(is_owner)
    def _():
        mine = pl.ds(pl.multiple_of(which * depth, depth), depth)
        cols = lanes_of(own_tile)
        whole = rate_ref[0:depth, cols]
        for n in range(1, len(OWNER_Z)):
            whole = jnp.where(which == n, rate_ref[n * depth : (n + 1) * depth, cols], whole)
        whole = jnp.exp(whole * (-2.0 * tokens / length))

        def send_back(p, to):
            @pl.when(to == me)
            def _():
                pltpu.make_async_copy(
                    prefix_ref.at[p], state_ref.at[mine, cols], state_sem.at[own_tile]
                ).start()

            @pl.when(to != me)
            def _():
                pltpu.make_async_remote_copy(
                    src_ref=prefix_ref.at[p],
                    dst_ref=state_ref.at[mine, cols],
                    send_sem=back_sem,
                    recv_sem=state_sem.at[own_tile],
                    device_id={"seq": to},
                    device_id_type=MESH,
                ).start()

        def group(n, total):
            some = pieces_ref.at[pl.ds(n * 4, 4)]
            pltpu.make_async_copy(some, some, piece_sem.at[n]).wait()

            def one(j, total):
                p = n * 4 + j
                prefix_ref[p] = total
                send_back(p, 2 * p)
                send_back(p, 2 * p + 1)
                return total * whole + pieces_ref[p]

            return lax.fori_loop(0, 4, one, total)

        lax.fori_loop(0, chips // 4, group, jnp.zeros((depth, LANES), F32))

    def add_state(n, carry):
        tile = near_first(n)
        cols = lanes_of(tile)
        arrived = state_ref.at[:, cols]
        pltpu.make_async_copy(arrived, arrived, state_sem.at[tile]).wait()
        keep = jnp.where(core == 1, decay_ref[4, :, cols], 1.0)
        start_ref[...] = state_ref[:, cols] * keep + other_ref[:, cols]
        eighth = [row(decay_ref.at[5], m, cols) for m in range(modes)]
        terms = [
            lead_ref[tile, m] * jnp.broadcast_to(start_ref[m : m + 1], (SUB, LANES))
            for m in range(modes)
        ]
        for i in range(steps):
            spots = pl.ds(i * SUB, SUB)
            total = list(terms)
            while len(total) > 1:
                total = [total[n] + total[n + 1] for n in range(0, len(total), 2)]
            mixed = q32_ref[tile, spots, :] * (y_ref[tile, spots, :] + total[0])
            y_ref[tile, spots, :] = mixed
            square_ref[spots, :] += mixed * mixed
            if i + 1 < steps:
                terms = [t * a for t, a in zip(terms, eighth)]
        return carry

    lax.fori_loop(0, tiles, add_state, 0)

    lanes = lax.broadcasted_iota(jnp.int32, (SUB, LANES), 1)
    part = jnp.zeros((SUB, LANES), F32)
    for i in range(steps):
        sums = jnp.sum(square_ref[i * SUB : (i + 1) * SUB, :], axis=1, keepdims=True)
        part = jnp.where(lanes == i, sums, part)
    part_ref[...] = part
    for n in (2, 1, 3):
        pltpu.make_async_remote_copy(
            src_ref=part_ref,
            dst_ref=parts_ref.at[n - 1],
            send_sem=part_send,
            recv_sem=part_sem,
            device_id={"chan": lax.rem(chan + n, chans)},
            device_id_type=MESH,
        ).start()
    pltpu.make_async_copy(parts_ref, parts_ref, part_sem).wait()
    whole_sum = part
    for n in range(1, chans):
        whole_sum = whole_sum + parts_ref[n - 1]
    scale = lax.rsqrt(whole_sum * (1.0 / (channels * chans)) + 1e-06)
    for i in range(steps):
        scale_ref[i * SUB : (i + 1) * SUB, :] = jnp.broadcast_to(scale[:, i : i + 1], (SUB, LANES))

    def finish(tile, carry):
        cols = lanes_of(tile)
        out_ref[:, cols] = (y_ref[tile] * scale_ref[...] * gain_ref[:, cols]).astype(out_ref.dtype)
        return carry

    lax.fori_loop(0, tiles, finish, 0)

    pltpu.make_async_copy(parts_ref, parts_ref, part_send).wait()

    @pl.when(core == 0)
    def _():
        pltpu.make_async_copy(local_ref, local_ref, send_sem).wait()

    @pl.when((core == 1) & is_owner)
    def _():
        sent = pieces_ref.at[pl.ds(0, pieces - 1)]
        pltpu.make_async_copy(sent, sent, send_sem).wait()

    @pl.when((core == 1) & jnp.logical_not(is_owner))
    def _():
        sent = pieces_ref.at[pl.ds(0, pieces)]
        pltpu.make_async_copy(sent, sent, send_sem).wait()

    @pl.when(is_owner)
    def _():
        most = prefix_ref.at[pl.ds(0, chips - 1)]
        pltpu.make_async_copy(prefix_ref, prefix_ref, back_sem).wait()
        pltpu.make_async_copy(most, most, back_sem).wait()


def per_device(devices, chans, q, k, v, residues, rates, skip, gain):
    tokens, channels = q.shape
    modes = residues.shape[1]
    tiles = channels // LANES
    chips = devices // 2
    bf16 = q.dtype
    inputs = (q, k, v, residues.T, rates.T, skip[None, :], gain[None, :])
    vmem = pltpu.VMEM
    dma = pltpu.SemaphoreType.DMA
    whole = vmem((tokens, channels), bf16)
    table = vmem((modes, channels), F32)
    line = vmem((1, channels), F32)
    by_tile = vmem((tiles, tokens, LANES), F32)
    by_mode = vmem((tiles, modes, SUB, LANES), F32)
    by_token = vmem((tokens, LANES), F32)
    by_chip = vmem((chips, modes // len(OWNER_Z), LANES), F32)
    return pl.pallas_call(
        functools.partial(body, float(tokens * devices)),
        out_shape=jax.ShapeDtypeStruct((tokens, channels), bf16),
        in_specs=[pl.BlockSpec(memory_space=pltpu.HBM)] * len(inputs),
        out_specs=pl.BlockSpec(memory_space=vmem),
        scratch_shapes=[whole, whole, whole, table, table, line, line]
        + [vmem((6, modes, channels), F32)]
        + [by_tile, by_tile, by_tile, by_mode, by_mode]
        + [table, table, table, table, vmem((modes, LANES), F32), by_token, by_token]
        + [by_chip, by_chip]
        + [vmem((SUB, LANES), F32), vmem((chans - 1, SUB, LANES), F32)]
        + [dma((5,)), dma((tiles // 2,)), dma((tiles // 2,)), dma((tiles,)), dma]
        + [dma((chips // 4,)), dma, dma((tiles,)), dma, dma],
        compiler_params=pltpu.CompilerParams(
            collective_id=0, has_side_effects=True, vmem_limit_bytes=24 * 1024 * 1024
        ),
    )(*[pltpu.with_memory_space_constraint(a, pltpu.HBM) for a in inputs])


def solution(mesh):
    devices, chans = mesh.shape["seq"], mesh.shape["chan"]
    return jax.shard_map(
        functools.partial(per_device, devices, chans),
        mesh=mesh,
        in_specs=(
            P("seq", "chan"),
            P("seq", "chan"),
            P("seq", "chan"),
            P("chan", None),
            P("chan", None),
            P("chan"),
            P("chan"),
        ),
        out_specs=P("seq", "chan"),
        check_vma=False,
    )
```

time: 29.7 us -> 25.1 us (0.85)
  the two profiles are of different devices: /device:TPU:1 before, /device:TPU:6 now
where the time goes in v2:
time: 25.1 us; the launch traced here: 25 us
  Pallas kernels  24.2 us (96%)
  local copies, waits for them, and re-layouts  0.8 us (3%)
    pallas_call x1, Pallas kernels, per_device(): pl.pallas_call(functools.partial(body, float(tokens * devices)), out_shap...  24.2 us
    unnamed x1, local copies, waits for them, and re-layouts  0.8 us

profile of v2, /device:TPU:6, one launch (start us, length us, event | category | flops | bytes accessed | tf_op | source)
XLA Modules:
  0.0 25.0 jit_solution(53420055093548431)
XLA Ops:
  0.0 24.2 %shard_map.73 = bf16[256,1024]{1,0:T(8,128)(2,1)S(1)} custom-call(bf16[256,1024]{1,0:T(8,128)(2,1)} %q_hbm.1, bf16[256,1024]{1,0:T(8,128)(2,1)} %k_hbm.1, bf16[256,1024]{1,0:T(8,128)(2,1)} %v_hbm.1, f32[16,1024]{1,0:T(8,128)} %bitcast.4, f32[16,1024]{1,0:T(8,128)} %bitcast.5, f32[1,1024]{1,0:T(1,128)} %bitcast.6, f32[1,1024]{1,0:T(1,128)} %bitcast.7), custom_call_target="tpu_custom_call" | custom-call | tf_op jit(solution)/shard_map/pallas_call | solution.py:413
  24.2 0.8 %copy.9 = bf16[256,1024]{1,0:T(8,128)(2,1)} copy(bf16[256,1024]{1,0:T(8,128)(2,1)S(1)} %shard_map.73) | data formatting | bytes 1048576

commit v3 on v2

v3 whole, which is shorter than its diff:
```python
import functools

import jax
import jax.numpy as jnp
from jax import lax
from jax.experimental import pallas as pl
from jax.experimental.pallas import tpu as pltpu
from jax.sharding import PartitionSpec as P

MESH = pl.DeviceIdType.MESH
F32 = jnp.float32
LANES = 128
SUB = 8
OWNER_Z = (0, 1)
DIRECT_Z = 4
QUIET = 5
POWERS = (1, 2, 4, 8, 16, 32, 64, 128, 256)


def shift_rows(x, n, rows):
    return jnp.where(rows >= n, pltpu.roll(x, n, 0), 0.0)


def body(
    length,
    q_hbm,
    k_hbm,
    v_hbm,
    res_hbm,
    rate_hbm,
    skip_hbm,
    gain_hbm,
    out_ref,
    q_ref,
    k_ref,
    v_ref,
    res_ref,
    rate_ref,
    skip_ref,
    gain_ref,
    decay_ref,
    g_ref,
    sorted_ref,
    y_ref,
    q32_ref,
    ends_ref,
    lead_ref,
    local_ref,
    other_ref,
    chip_ref,
    state_ref,
    start_ref,
    square_ref,
    pieces_ref,
    prefix_ref,
    part_ref,
    parts_ref,
    load_sem,
    key_sem,
    value_sem,
    other_sem,
    pair_sem,
    send_sem,
    piece_sem,
    back_sem,
    state_sem,
    part_send,
    part_sem,
):
    me = lax.axis_index("seq")
    chan = lax.axis_index("chan")
    tokens, channels = q_ref.shape
    modes = res_ref.shape[0]
    tiles = channels // LANES
    steps = tokens // SUB
    sub = tokens // SUB
    chips = pieces_ref.shape[0]
    devices = 2 * chips
    chans = parts_ref.shape[0] + 1
    chip = me // 2
    x, z, core = me // 16, lax.rem(chip, 8), lax.rem(me, 2)
    is_owner = (z == OWNER_Z[0]) | (z == OWNER_Z[1])
    which = jnp.where(z == OWNER_Z[1], 1, 0)
    own_tile = 2 * x + core
    depth = modes // 2
    direct = z < DIRECT_Z

    def owner_of(half, tile):
        return ((tile // 2) * 8 + OWNER_Z[half]) * 2 + lax.rem(tile, 2)

    def far_first(n):
        pair = n // 2
        turn = jnp.where(pair == 0, 2, jnp.where(pair == 1, 1, jnp.where(pair == 2, 3, 0)))
        return lax.rem(x + turn, 4) * 2 + lax.rem(n, 2)

    def near_first(n):
        pair = n // 2
        turn = jnp.where(pair == 1, 3, jnp.where(pair == 2, 1, jnp.where(pair == 3, 2, 0)))
        return lax.rem(x + turn, 4) * 2 + lax.rem(n, 2)

    def lanes_of(tile, width=1):
        return pl.ds(pl.multiple_of(tile * LANES, LANES), width * LANES)

    def load(src, dst, sem):
        return pltpu.make_async_copy(src, dst, sem)

    rate_load = load(rate_hbm, rate_ref, load_sem.at[0])
    rate_load.start()

    def load_pair(pair):
        cols = lanes_of(far_first(2 * pair), 2)
        return (
            load(k_hbm.at[:, cols], k_ref.at[:, cols], key_sem.at[pair]),
            load(v_hbm.at[:, cols], v_ref.at[:, cols], value_sem.at[pair]),
        )

    for pair in range(tiles // 2):
        for copy in load_pair(pair):
            copy.start()
    late_loads = [
        load(src, dst, load_sem.at[n + 1])
        for n, (src, dst) in enumerate(
            ((res_hbm, res_ref), (q_hbm, q_ref), (skip_hbm, skip_ref), (gain_hbm, gain_ref))
        )
    ]
    for copy in late_loads:
        copy.start()

    barrier = pltpu.get_barrier_semaphore()

    @pl.when(is_owner)
    def _():
        def greet(n, carry):
            sender = lax.rem(chip + n, chips)

            @pl.when(2 * sender != me)
            def _():
                pl.semaphore_signal(
                    barrier, inc=1, device_id={"seq": 2 * sender}, device_id_type=MESH
                )

            return carry

        lax.fori_loop(0, chips, greet, 0)

    @pl.when(core == 0)
    def _():
        pl.semaphore_signal(barrier, inc=1, device_id={"seq": me + 1}, device_id_type=MESH)

    for n in range(1, chans):
        pl.semaphore_signal(
            barrier, inc=1, device_id={"chan": lax.rem(chan + n, chans)}, device_id_type=MESH
        )

    rows = lax.broadcasted_iota(jnp.int32, (SUB, LANES), 0)
    rows_f = rows.astype(F32)

    def set_decay(power):
        for tile in range(tiles):
            rate = rate_ref[:, tile * LANES : (tile + 1) * LANES]
            decay_ref[POWERS.index(power), tile] = jnp.exp(rate * (-float(power) / length))

    rate_load.wait()
    for power in (1, 2, 4, 8, 16):
        set_decay(power)

    def row(ref, m, cols):
        return jnp.broadcast_to(ref[m : m + 1, cols], (SUB, LANES))

    def decay_row(power, tile, m):
        return jnp.broadcast_to(decay_ref[POWERS.index(power), tile, m : m + 1], (SUB, LANES))


    def wait_pair(n):
        @pl.when(lax.rem(n, 2) == 0)
        def _():
            for copy in load_pair(n // 2):
                copy.wait()

    def run_block(n):
        tile = far_first(n)
        cols = lanes_of(tile)
        eighth = [decay_row(8, tile, m) for m in range(modes)]
        stride = [decay_row(16, tile, m) for m in range(modes)]
        held = None
        for i in range(0, tokens, 2 * SUB):
            spots = slice(i, i + 2 * SUB)
            g = k_ref[spots, cols].astype(F32) * v_ref[spots, cols].astype(F32)
            step = [g[:SUB] * a + g[SUB:] for a in eighth]
            held = step if held is None else [h * a + t for h, a, t in zip(held, stride, step)]
        for m in range(modes):
            ends_ref[tile, m] = held[m]

    def gather_rows(n):
        tile = far_first(n)
        for m in range(modes):
            end = ends_ref[tile, m]
            for power in (1, 2, 4):
                end = end + decay_row(power, tile, m) * pltpu.roll(end, power, 0)
            local_ref[tile, m : m + 1] = end[SUB - 1 :]

    def send_local(n):
        tile = far_first(n)

        @pl.when(core == 1)
        def _():
            pltpu.make_async_remote_copy(
                src_ref=local_ref.at[tile],
                dst_ref=other_ref.at[tile],
                send_sem=pair_sem,
                recv_sem=other_sem.at[tile],
                device_id={"seq": me - 1},
                device_id_type=MESH,
            ).start()

    def quiet_block(n, carry):
        wait_pair(n)
        gather_rows(n - 1)
        run_block(n)
        return carry

    def sending_block(n, carry):
        quiet_block(n, carry)
        send_local(n - 1)
        return carry

    def send_earlier(n, carry):
        send_local(n)
        return carry

    wait_pair(0)
    run_block(0)
    lax.fori_loop(1, QUIET, quiet_block, 0)
    sends = 2 * tiles - jnp.where(is_owner, 1, 0)
    pl.semaphore_wait(barrier, chans - 1 + jnp.where(core == 0, sends, 1))
    lax.fori_loop(0, QUIET - 1, send_earlier, 0)
    lax.fori_loop(QUIET, tiles, sending_block, 0)
    gather_rows(tiles - 1)
    send_local(tiles - 1)

    set_decay(tokens)

    @pl.when(core == 0)
    def _():
        def send_pieces(n, carry):
            tile = far_first(n)
            mine = other_ref.at[tile]
            pltpu.make_async_copy(mine, mine, other_sem.at[tile]).wait()
            chip_ref[tile] = local_ref[tile] * decay_ref[POWERS.index(tokens), tile] + other_ref[tile]
            for half in range(2):
                owner = owner_of(half, tile)
                piece = chip_ref.at[tile, half * depth : (half + 1) * depth]

                @pl.when((owner == me))
                def _():
                    pltpu.make_async_copy(
                        piece, pieces_ref.at[chip], piece_sem.at[chip // 4]
                    ).start()

                @pl.when((owner != me))
                def _():
                    pltpu.make_async_remote_copy(
                        src_ref=piece,
                        dst_ref=pieces_ref.at[chip],
                        send_sem=send_sem,
                        recv_sem=piece_sem.at[chip // 4],
                        device_id={"seq": owner},
                        device_id_type=MESH,
                    ).start()

            return carry

        lax.fori_loop(0, tiles, send_pieces, 0)
        pltpu.make_async_remote_copy(
            src_ref=local_ref,
            dst_ref=other_ref,
            send_sem=pair_sem,
            recv_sem=other_sem.at[0],
            device_id={"seq": me + 1},
            device_id_type=MESH,
        ).start()

    for copy in late_loads:
        copy.wait()
    for power in (32, 64, 128):
        set_decay(power)

    def local_part(tile, carry):
        cols = lanes_of(tile)
        q32_ref[tile] = q_ref[:, cols].astype(F32)
        g_ref[...] = k_ref[:, cols].astype(F32) * v_ref[:, cols].astype(F32)
        decay = [decay_row(1, tile, m) for m in range(modes)]
        stride = [decay_row(4, tile, m) for m in range(modes)]
        held = None
        for i in range(0, sub, 4):
            g = [g_ref[pl.ds(i + j, SUB, stride=sub), :] for j in range(4)]
            for j in range(4):
                sorted_ref[(i + j) * SUB : (i + j + 1) * SUB, :] = g[j]
            step = [((g[0] * a + g[1]) * a + g[2]) * a + g[3] for a in decay]
            held = step if held is None else [h * a + t for h, a, t in zip(held, stride, step)]
        for m in range(modes):
            rate = row(rate_ref, m, cols) * (-1.0 / length)
            lead_ref[tile, m] = row(res_ref, m, cols) * jnp.exp(rate * (rows_f + 1.0))
            for n in (1, 2, 4):
                held[m] = held[m] + decay_row(n * sub, tile, m) * shift_rows(held[m], n, rows)
            held[m] = shift_rows(held[m], 1, rows)
        weight = [row(res_ref, m, cols) for m in range(modes)]
        skip = row(skip_ref, 0, cols)
        for i in range(sub):
            spots = pl.ds(i, SUB, stride=sub)
            g = sorted_ref[i * SUB : (i + 1) * SUB, :]
            held = [h * a + g for h, a in zip(held, decay)]
            terms = [h * w for h, w in zip(held, weight)] + [skip * g]
            while len(terms) > 1:
                terms = [sum(terms[n : n + 2]) for n in range(0, len(terms), 2)]
            y_ref[tile, spots, :] = terms[0]
        return carry

    lax.fori_loop(0, tiles, local_part, 0)
    square_ref[...] = jnp.zeros_like(square_ref)

    @pl.when(is_owner)
    def _():
        mine = pl.ds(pl.multiple_of(which * depth, depth), depth)
        whole = jnp.exp(rate_ref[mine, lanes_of(own_tile)] * (-2.0 * tokens / length))

        def send_back(p, to):
            @pl.when(to == me)
            def _():
                pltpu.make_async_copy(
                    prefix_ref.at[p], state_ref.at[own_tile, mine], state_sem.at[own_tile]
                ).start()

            @pl.when(to != me)
            def _():
                pltpu.make_async_remote_copy(
                    src_ref=prefix_ref.at[p],
                    dst_ref=state_ref.at[own_tile, mine],
                    send_sem=back_sem,
                    recv_sem=state_sem.at[own_tile],
                    device_id={"seq": to},
                    device_id_type=MESH,
                ).start()

        def give(p, total):
            prefix_ref[p] = total
            send_back(p, 2 * p)

            @pl.when(lax.rem(p, 8) < DIRECT_Z)
            def _():
                send_back(p, 2 * p + 1)

        nothing = jnp.zeros((depth, LANES), F32)

        def group(n, total):
            some = pieces_ref.at[pl.ds(n * 4, 4)]
            pltpu.make_async_copy(some, some, piece_sem.at[n]).wait()
            give(n * 4, total)

            def one(j, total):
                p = n * 4 + j
                total = total * whole + pieces_ref[p]

                @pl.when(j < 3)
                def _():
                    give(p + 1, total)

                return total

            return lax.fori_loop(0, 4, one, total)

        lax.fori_loop(0, chips // 4, group, nothing)

    @pl.when(core == 1)
    def _():
        pltpu.make_async_copy(other_ref, other_ref, other_sem.at[0]).wait()

    def add_state(n, carry):
        tile = near_first(n)
        cols = lanes_of(tile)
        arrived = state_ref.at[tile]
        pltpu.make_async_copy(arrived, arrived, state_sem.at[tile]).wait()

        @pl.when((core == 0) & jnp.logical_not(direct))
        def _():
            pltpu.make_async_remote_copy(
                src_ref=state_ref.at[tile],
                dst_ref=state_ref.at[tile],
                send_sem=pair_sem,
                recv_sem=state_sem.at[tile],
                device_id={"seq": me + 1},
                device_id_type=MESH,
            ).start()

        state = state_ref[tile]
        start_ref[...] = jnp.where(core == 1, state * decay_ref[POWERS.index(tokens), tile] + other_ref[tile], state)
        gain = row(gain_ref, 0, cols)
        eighth = [decay_row(SUB, tile, m) for m in range(modes)]
        terms = [
            lead_ref[tile, m] * jnp.broadcast_to(start_ref[m : m + 1], (SUB, LANES))
            for m in range(modes)
        ]
        for i in range(steps):
            spots = pl.ds(i * SUB, SUB)
            total = list(terms)
            while len(total) > 1:
                total = [total[n] + total[n + 1] for n in range(0, len(total), 2)]
            mixed = q32_ref[tile, spots, :] * (y_ref[tile, spots, :] + total[0])
            y_ref[tile, spots, :] = mixed * gain
            square_ref[spots, :] += mixed * mixed
            if i + 1 < steps:
                terms = [t * a for t, a in zip(terms, eighth)]
        return carry

    lax.fori_loop(0, tiles, add_state, 0)

    lanes = lax.broadcasted_iota(jnp.int32, (SUB, LANES), 1)
    part = jnp.zeros((SUB, LANES), F32)
    for i in range(steps):
        sums = jnp.sum(square_ref[i * SUB : (i + 1) * SUB, :], axis=1, keepdims=True)
        part = jnp.where(lanes == i, sums, part)
    part_ref[...] = part
    for n in (2, 1, 3):
        pltpu.make_async_remote_copy(
            src_ref=part_ref,
            dst_ref=parts_ref.at[n - 1],
            send_sem=part_send,
            recv_sem=part_sem,
            device_id={"chan": lax.rem(chan + n, chans)},
            device_id_type=MESH,
        ).start()
    pltpu.make_async_copy(parts_ref, parts_ref, part_sem).wait()
    whole_sum = part
    for n in range(1, chans):
        whole_sum = whole_sum + parts_ref[n - 1]
    scale = lax.rsqrt(whole_sum * (1.0 / (channels * chans)) + 1e-06)
    for i in range(0, steps, 2):
        above = jnp.broadcast_to(scale[:, i : i + 1], (SUB, LANES))
        below = jnp.broadcast_to(scale[:, i + 1 : i + 2], (SUB, LANES))
        both = jnp.concatenate([above, below], axis=0)
        spots = slice(i * SUB, (i + 2) * SUB)
        for tile in range(tiles):
            cols = slice(tile * LANES, (tile + 1) * LANES)
            out_ref[spots, cols] = (y_ref[tile, spots, :] * both).astype(out_ref.dtype)

    pltpu.make_async_copy(parts_ref, parts_ref, part_send).wait()

    pltpu.make_async_copy(local_ref, local_ref, pair_sem).wait()

    @pl.when((core == 0) & jnp.logical_not(direct))
    def _():
        pltpu.make_async_copy(state_ref, state_ref, pair_sem).wait()

    def sent(count, sem):
        some = prefix_ref.at[pl.ds(0, count)]
        pltpu.make_async_copy(some, some, sem).wait()

    @pl.when((core == 0) & is_owner)
    def _():
        sent(2 * tiles - 1, send_sem)

    @pl.when((core == 0) & jnp.logical_not(is_owner))
    def _():
        sent(2 * tiles, send_sem)

    @pl.when(is_owner)
    def _():
        sent(chips - 1, back_sem)
        sent(4 * DIRECT_Z, back_sem)


def per_device(devices, chans, q, k, v, residues, rates, skip, gain):
    tokens, channels = q.shape
    modes = residues.shape[1]
    tiles = channels // LANES
    chips = devices // 2
    bf16 = q.dtype
    inputs = (q, k, v, residues.T, rates.T, skip[None, :], gain[None, :])
    vmem = pltpu.VMEM
    dma = pltpu.SemaphoreType.DMA
    whole = vmem((tokens, channels), bf16)
    table = vmem((modes, channels), F32)
    line = vmem((1, channels), F32)
    by_tile = vmem((tiles, tokens, LANES), F32)
    by_mode = vmem((tiles, modes, SUB, LANES), F32)
    by_token = vmem((tokens, LANES), F32)
    by_chip = vmem((chips, modes // 2, LANES), F32)
    packed = vmem((tiles, modes, LANES), F32)
    return pl.pallas_call(
        functools.partial(body, float(tokens * devices)),
        out_shape=jax.ShapeDtypeStruct((tokens, channels), bf16),
        in_specs=[pl.BlockSpec(memory_space=pltpu.HBM)] * len(inputs),
        out_specs=pl.BlockSpec(memory_space=vmem),
        scratch_shapes=[whole, whole, whole, table, table, line, line]
        + [vmem((len(POWERS), tiles, modes, LANES), F32)]
        + [by_token, by_token, by_tile, by_tile, by_mode, by_mode]
        + [packed, packed, packed, packed, vmem((modes, LANES), F32), by_token]
        + [by_chip, by_chip]
        + [vmem((SUB, LANES), F32), vmem((chans - 1, SUB, LANES), F32)]
        + [dma((5,)), dma((tiles // 2,)), dma((tiles // 2,)), dma((tiles,)), dma, dma]
        + [dma((chips // 4,)), dma, dma((tiles,)), dma, dma],
        compiler_params=pltpu.CompilerParams(
            collective_id=0, has_side_effects=True, vmem_limit_bytes=24 * 1024 * 1024
        ),
    )(*[pltpu.with_memory_space_constraint(a, pltpu.HBM) for a in inputs])


def solution(mesh):
    devices, chans = mesh.shape["seq"], mesh.shape["chan"]
    return jax.shard_map(
        functools.partial(per_device, devices, chans),
        mesh=mesh,
        in_specs=(
            P("seq", "chan"),
            P("seq", "chan"),
            P("seq", "chan"),
            P("chan", None),
            P("chan", None),
            P("chan"),
            P("chan"),
        ),
        out_specs=P("seq", "chan"),
        check_vma=False,
    )
```

time: 25.1 us -> 24.1 us (0.960)
  Pallas kernels: 24.2 us -> 23.2 us
    pallas_call x1, Pallas kernels: 24.2 us -> 23.2 us  [per_device(): pl.pallas_call(functools.partial(body, float(tokens * devices)), out_shap...]
where the time goes in v3:
time: 24.1 us; the launch traced here: 24 us
  Pallas kernels  23.2 us (96%)
  local copies, waits for them, and re-layouts  0.8 us (3%)
    pallas_call x1, Pallas kernels, per_device(): pl.pallas_call(functools.partial(body, float(tokens * devices)), out_shap...  23.2 us
    unnamed x1, local copies, waits for them, and re-layouts  0.8 us

profile of v3, /device:TPU:6, one launch (start us, length us, event | category | flops | bytes accessed | tf_op | source)
XLA Modules:
  0.0 24.0 jit_solution(12621522190098895711)
XLA Ops:
  0.0 23.2 %shard_map.73 = bf16[256,1024]{1,0:T(8,128)(2,1)S(1)} custom-call(bf16[256,1024]{1,0:T(8,128)(2,1)} %q_hbm.1, bf16[256,1024]{1,0:T(8,128)(2,1)} %k_hbm.1, bf16[256,1024]{1,0:T(8,128)(2,1)} %v_hbm.1, f32[16,1024]{1,0:T(8,128)} %bitcast.4, f32[16,1024]{1,0:T(8,128)} %bitcast.5, f32[1,1024]{1,0:T(1,128)} %bitcast.6, f32[1,1024]{1,0:T(1,128)} %bitcast.7), custom_call_target="tpu_custom_call" | custom-call | tf_op jit(solution)/shard_map/pallas_call | solution.py:489
  23.2 0.8 %copy.9 = bf16[256,1024]{1,0:T(8,128)(2,1)} copy(bf16[256,1024]{1,0:T(8,128)(2,1)S(1)} %shard_map.73) | data formatting | bytes 1048576

commit v4 on v3

--- a/solution.py
+++ b/solution.py
@@ -13,7 +13,7 @@
 SUB = 8
 OWNER_Z = (0, 1)
 DIRECT_Z = 4
-QUIET = 5
+QUIET = 4
 POWERS = (1, 2, 4, 8, 16, 32, 64, 128, 256)
 
 
@@ -75,14 +75,15 @@
     steps = tokens // SUB
     sub = tokens // SUB
     chips = pieces_ref.shape[0]
-    devices = 2 * chips
+    groups = chips // 4
     chans = parts_ref.shape[0] + 1
     chip = me // 2
     x, z, core = me // 16, lax.rem(chip, 8), lax.rem(me, 2)
-    is_owner = (z == OWNER_Z[0]) | (z == OWNER_Z[1])
-    which = jnp.where(z == OWNER_Z[1], 1, 0)
+    parties = len(OWNER_Z)
+    is_owner = (z == OWNER_Z[0]) | (z == OWNER_Z[-1])
+    which = jnp.where(z == OWNER_Z[0], 0, parties - 1)
     own_tile = 2 * x + core
-    depth = modes // 2
+    depth = modes // parties
     direct = z < DIRECT_Z
 
     def owner_of(half, tile):
@@ -90,7 +91,7 @@
 
     def far_first(n):
         pair = n // 2
-        turn = jnp.where(pair == 0, 2, jnp.where(pair == 1, 1, jnp.where(pair == 2, 3, 0)))
+        turn = jnp.where(pair == 0, 2, jnp.where(pair == 1, 3, jnp.where(pair == 2, 1, 0)))
         return lax.rem(x + turn, 4) * 2 + lax.rem(n, 2)
 
     def near_first(n):
@@ -103,9 +104,6 @@
 
     def load(src, dst, sem):
         return pltpu.make_async_copy(src, dst, sem)
-
-    rate_load = load(rate_hbm, rate_ref, load_sem.at[0])
-    rate_load.start()
 
     def load_pair(pair):
         cols = lanes_of(far_first(2 * pair), 2)
@@ -114,17 +112,11 @@
             load(v_hbm.at[:, cols], v_ref.at[:, cols], value_sem.at[pair]),
         )
 
+    rate_load = load(rate_hbm, rate_ref, load_sem.at[0])
+    rate_load.start()
     for pair in range(tiles // 2):
         for copy in load_pair(pair):
             copy.start()
-    late_loads = [
-        load(src, dst, load_sem.at[n + 1])
-        for n, (src, dst) in enumerate(
-            ((res_hbm, res_ref), (q_hbm, q_ref), (skip_hbm, skip_ref), (gain_hbm, gain_ref))
-        )
-    ]
-    for copy in late_loads:
-        copy.start()
 
     barrier = pltpu.get_barrier_semaphore()
 
@@ -161,7 +153,7 @@
             decay_ref[POWERS.index(power), tile] = jnp.exp(rate * (-float(power) / length))
 
     rate_load.wait()
-    for power in (1, 2, 4, 8, 16):
+    for power in (1, 2, 4, 8, 16, tokens):
         set_decay(power)
 
     def row(ref, m, cols):
@@ -213,6 +205,32 @@
                 device_id_type=MESH,
             ).start()
 
+    def send_piece(n, carry):
+        tile = far_first(n)
+        mine = other_ref.at[tile]
+        pltpu.make_async_copy(mine, mine, other_sem.at[tile]).wait()
+        chip_ref[tile] = local_ref[tile] * decay_ref[POWERS.index(tokens), tile] + other_ref[tile]
+        for half in range(parties):
+            owner = owner_of(half, tile)
+            piece = chip_ref.at[tile, half * depth : (half + 1) * depth]
+
+            @pl.when(owner == me)
+            def _():
+                pltpu.make_async_copy(piece, pieces_ref.at[chip], piece_sem.at[chip // 4]).start()
+
+            @pl.when(owner != me)
+            def _():
+                pltpu.make_async_remote_copy(
+                    src_ref=piece,
+                    dst_ref=pieces_ref.at[chip],
+                    send_sem=send_sem,
+                    recv_sem=piece_sem.at[chip // 4],
+                    device_id={"seq": owner},
+                    device_id_type=MESH,
+                ).start()
+
+        return carry
+
     def quiet_block(n, carry):
         wait_pair(n)
         gather_rows(n - 1)
@@ -222,55 +240,38 @@
     def sending_block(n, carry):
         quiet_block(n, carry)
         send_local(n - 1)
+
+        @pl.when(core == 0)
+        def _():
+            send_piece(n - QUIET, 0)
+
         return carry
 
     def send_earlier(n, carry):
         send_local(n)
         return carry
 
+    late_loads = [
+        load(src, dst, load_sem.at[n + 1])
+        for n, (src, dst) in enumerate(
+            ((res_hbm, res_ref), (q_hbm, q_ref), (skip_hbm, skip_ref), (gain_hbm, gain_ref))
+        )
+    ]
+    for copy in late_loads:
+        copy.start()
     wait_pair(0)
     run_block(0)
     lax.fori_loop(1, QUIET, quiet_block, 0)
-    sends = 2 * tiles - jnp.where(is_owner, 1, 0)
+    sends = parties * tiles - jnp.where(is_owner, 1, 0)
     pl.semaphore_wait(barrier, chans - 1 + jnp.where(core == 0, sends, 1))
     lax.fori_loop(0, QUIET - 1, send_earlier, 0)
     lax.fori_loop(QUIET, tiles, sending_block, 0)
     gather_rows(tiles - 1)
     send_local(tiles - 1)
 
-    set_decay(tokens)
-
     @pl.when(core == 0)
     def _():
-        def send_pieces(n, carry):
-            tile = far_first(n)
-            mine = other_ref.at[tile]
-            pltpu.make_async_copy(mine, mine, other_sem.at[tile]).wait()
-            chip_ref[tile] = local_ref[tile] * decay_ref[POWERS.index(tokens), tile] + other_ref[tile]
-            for half in range(2):
-                owner = owner_of(half, tile)
-                piece = chip_ref.at[tile, half * depth : (half + 1) * depth]
-
-                @pl.when((owner == me))
-                def _():
-                    pltpu.make_async_copy(
-                        piece, pieces_ref.at[chip], piece_sem.at[chip // 4]
-                    ).start()
-
-                @pl.when((owner != me))
-                def _():
-                    pltpu.make_async_remote_copy(
-                        src_ref=piece,
-                        dst_ref=pieces_ref.at[chip],
-                        send_sem=send_sem,
-                        recv_sem=piece_sem.at[chip // 4],
-                        device_id={"seq": owner},
-                        device_id_type=MESH,
-                    ).start()
-
-            return carry
-
-        lax.fori_loop(0, tiles, send_pieces, 0)
+        lax.fori_loop(tiles - QUIET, tiles, send_piece, 0)
         pltpu.make_async_remote_copy(
             src_ref=local_ref,
             dst_ref=other_ref,
@@ -342,34 +343,41 @@
                     device_id_type=MESH,
                 ).start()
 
-        def give(p, total):
-            prefix_ref[p] = total
-            send_back(p, 2 * p)
-
-            @pl.when(lax.rem(p, 8) < DIRECT_Z)
-            def _():
-                send_back(p, 2 * p + 1)
-
-        nothing = jnp.zeros((depth, LANES), F32)
-
-        def group(n, total):
+        def give_group(n):
+            for j in range(4):
+                p = n * 4 + j
+                send_back(p, 2 * p)
+
+                @pl.when(lax.rem(p, 8) < DIRECT_Z)
+                def _():
+                    send_back(p, 2 * p + 1)
+
+        def take_group(n, total):
+            for j in range(4):
+                prefix_ref[n * 4 + j] = total
+                total = total * whole + pieces_ref[n * 4 + j]
+            return total
+
+        def await_group(n):
             some = pieces_ref.at[pl.ds(n * 4, 4)]
             pltpu.make_async_copy(some, some, piece_sem.at[n]).wait()
-            give(n * 4, total)
-
-            def one(j, total):
-                p = n * 4 + j
-                total = total * whole + pieces_ref[p]
-
-                @pl.when(j < 3)
-                def _():
-                    give(p + 1, total)
-
-                return total
-
-            return lax.fori_loop(0, 4, one, total)
-
-        lax.fori_loop(0, chips // 4, group, nothing)
+
+        for line in range(groups // 2):
+            await_group(2 * line)
+
+        def one_line(line, total):
+            total = take_group(2 * line, total)
+            give_group(2 * line)
+
+            @pl.when(line > 0)
+            def _():
+                give_group(2 * line - 1)
+
+            await_group(2 * line + 1)
+            return take_group(2 * line + 1, total)
+
+        lax.fori_loop(0, groups // 2, one_line, jnp.zeros((depth, LANES), F32))
+        give_group(groups - 1)
 
     @pl.when(core == 1)
     def _():
@@ -457,11 +465,11 @@
 
     @pl.when((core == 0) & is_owner)
     def _():
-        sent(2 * tiles - 1, send_sem)
+        sent(parties * tiles - 1, send_sem)
 
     @pl.when((core == 0) & jnp.logical_not(is_owner))
     def _():
-        sent(2 * tiles, send_sem)
+        sent(parties * tiles, send_sem)
 
     @pl.when(is_owner)
     def _():
@@ -484,7 +492,7 @@
     by_tile = vmem((tiles, tokens, LANES), F32)
     by_mode = vmem((tiles, modes, SUB, LANES), F32)
     by_token = vmem((tokens, LANES), F32)
-    by_chip = vmem((chips, modes // 2, LANES), F32)
+    by_chip = vmem((chips, modes // len(OWNER_Z), LANES), F32)
     packed = vmem((tiles, modes, LANES), F32)
     return pl.pallas_call(
         functools.partial(body, float(tokens * devices)),

time: 24.1 us -> 23.5 us (0.975)
  Pallas kernels: 23.2 us -> 22.6 us
    pallas_call x1, Pallas kernels: 23.2 us -> 22.6 us  [per_device(): pl.pallas_call(functools.partial(body, float(tokens * devices)), out_shap...]
where the time goes in v4:
time: 23.5 us; the launch traced here: 23.4 us
  Pallas kernels  22.6 us (96%)
  local copies, waits for them, and re-layouts  0.8 us (3%)
    pallas_call x1, Pallas kernels, per_device(): pl.pallas_call(functools.partial(body, float(tokens * devices)), out_shap...  22.6 us
    unnamed x1, local copies, waits for them, and re-layouts  0.8 us

profile of v4, /device:TPU:6, one launch (start us, length us, event | category | flops | bytes accessed | tf_op | source)
XLA Modules:
  0.0 23.4 jit_solution(3705063279624549965)
XLA Ops:
  0.0 22.6 %shard_map.73 = bf16[256,1024]{1,0:T(8,128)(2,1)S(1)} custom-call(bf16[256,1024]{1,0:T(8,128)(2,1)} %q_hbm.1, bf16[256,1024]{1,0:T(8,128)(2,1)} %k_hbm.1, bf16[256,1024]{1,0:T(8,128)(2,1)} %v_hbm.1, f32[16,1024]{1,0:T(8,128)} %bitcast.4, f32[16,1024]{1,0:T(8,128)} %bitcast.5, f32[1,1024]{1,0:T(1,128)} %bitcast.6, f32[1,1024]{1,0:T(1,128)} %bitcast.7), custom_call_target="tpu_custom_call" | custom-call | tf_op jit(solution)/shard_map/pallas_call | solution.py:497
  22.6 0.8 %copy.9 = bf16[256,1024]{1,0:T(8,128)(2,1)} copy(bf16[256,1024]{1,0:T(8,128)(2,1)S(1)} %shard_map.73) | data formatting | bytes 1048576

commit v5 on v4

--- a/solution.py
+++ b/solution.py
@@ -12,7 +12,7 @@
 LANES = 128
 SUB = 8
 OWNER_Z = (0, 1)
-DIRECT_Z = 4
+DIRECT_Z = 3
 QUIET = 4
 POWERS = (1, 2, 4, 8, 16, 32, 64, 128, 256)
 
@@ -343,20 +343,25 @@
                     device_id_type=MESH,
                 ).start()
 
+        def give(p):
+            send_back(p, 2 * p)
+
+            @pl.when(lax.rem(p, 8) < DIRECT_Z)
+            def _():
+                send_back(p, 2 * p + 1)
+
+        def take_group(n, total, at_once):
+            for j in range(4):
+                p = n * 4 + j
+                prefix_ref[p] = total
+                if at_once:
+                    give(p)
+                total = total * whole + pieces_ref[p]
+            return total
+
         def give_group(n):
             for j in range(4):
-                p = n * 4 + j
-                send_back(p, 2 * p)
-
-                @pl.when(lax.rem(p, 8) < DIRECT_Z)
-                def _():
-                    send_back(p, 2 * p + 1)
-
-        def take_group(n, total):
-            for j in range(4):
-                prefix_ref[n * 4 + j] = total
-                total = total * whole + pieces_ref[n * 4 + j]
-            return total
+                give(n * 4 + j)
 
         def await_group(n):
             some = pieces_ref.at[pl.ds(n * 4, 4)]
@@ -366,15 +371,18 @@
             await_group(2 * line)
 
         def one_line(line, total):
-            total = take_group(2 * line, total)
-            give_group(2 * line)
-
-            @pl.when(line > 0)
+            @pl.when(line == 1)
             def _():
                 give_group(2 * line - 1)
 
+            total = take_group(2 * line, total, True)
+
+            @pl.when(line > 1)
+            def _():
+                give_group(2 * line - 1)
+
             await_group(2 * line + 1)
-            return take_group(2 * line + 1, total)
+            return take_group(2 * line + 1, total, False)
 
         lax.fori_loop(0, groups // 2, one_line, jnp.zeros((depth, LANES), F32))
         give_group(groups - 1)

time: 23.5 us -> 23.5 us (level)
  no operation moved by 1% of the time
where the time goes in v5:
time: 23.5 us; the launch traced here: 23.4 us
  Pallas kernels  22.6 us (96%)
  local copies, waits for them, and re-layouts  0.8 us (3%)
    pallas_call x1, Pallas kernels, per_device(): pl.pallas_call(functools.partial(body, float(tokens * devices)), out_shap...  22.6 us
    unnamed x1, local copies, waits for them, and re-layouts  0.8 us

profile of v5, /device:TPU:6, one launch (start us, length us, event | category | flops | bytes accessed | tf_op | source)
XLA Modules:
  0.0 23.4 jit_solution(15220949544158479697)
XLA Ops:
  0.0 22.6 %shard_map.73 = bf16[256,1024]{1,0:T(8,128)(2,1)S(1)} custom-call(bf16[256,1024]{1,0:T(8,128)(2,1)} %q_hbm.1, bf16[256,1024]{1,0:T(8,128)(2,1)} %k_hbm.1, bf16[256,1024]{1,0:T(8,128)(2,1)} %v_hbm.1, f32[16,1024]{1,0:T(8,128)} %bitcast.4, f32[16,1024]{1,0:T(8,128)} %bitcast.5, f32[1,1024]{1,0:T(1,128)} %bitcast.6, f32[1,1024]{1,0:T(1,128)} %bitcast.7), custom_call_target="tpu_custom_call" | custom-call | tf_op jit(solution)/shard_map/pallas_call | solution.py:505
  22.6 0.8 %copy.9 = bf16[256,1024]{1,0:T(8,128)(2,1)} copy(bf16[256,1024]{1,0:T(8,128)(2,1)S(1)} %shard_map.73) | data formatting | bytes 1048576

commit v6 on v5

--- a/solution.py
+++ b/solution.py
@@ -30,7 +30,8 @@
     rate_hbm,
     skip_hbm,
     gain_hbm,
-    out_ref,
+    y_ref,
+    scale_ref,
     q_ref,
     k_ref,
     v_ref,
@@ -41,7 +42,6 @@
     decay_ref,
     g_ref,
     sorted_ref,
-    y_ref,
     q32_ref,
     ends_ref,
     lead_ref,
@@ -450,14 +450,7 @@
     for n in range(1, chans):
         whole_sum = whole_sum + parts_ref[n - 1]
     scale = lax.rsqrt(whole_sum * (1.0 / (channels * chans)) + 1e-06)
-    for i in range(0, steps, 2):
-        above = jnp.broadcast_to(scale[:, i : i + 1], (SUB, LANES))
-        below = jnp.broadcast_to(scale[:, i + 1 : i + 2], (SUB, LANES))
-        both = jnp.concatenate([above, below], axis=0)
-        spots = slice(i * SUB, (i + 2) * SUB)
-        for tile in range(tiles):
-            cols = slice(tile * LANES, (tile + 1) * LANES)
-            out_ref[spots, cols] = (y_ref[tile, spots, :] * both).astype(out_ref.dtype)
+    scale_ref[...] = scale
 
     pltpu.make_async_copy(parts_ref, parts_ref, part_send).wait()
 
@@ -483,6 +476,28 @@
     def _():
         sent(chips - 1, back_sem)
         sent(4 * DIRECT_Z, back_sem)
+
+
+def finish(y_ref, scale_ref, out_hbm, out_ref, sems):
+    tiles, tokens, _ = y_ref.shape
+    chunk = tokens // sems.shape[0]
+    scale = scale_ref[...]
+    copies = []
+    for n in range(sems.shape[0]):
+        for i in range(n * chunk, (n + 1) * chunk, 2 * SUB):
+            lane = i // SUB
+            above = jnp.broadcast_to(scale[:, lane : lane + 1], (SUB, LANES))
+            below = jnp.broadcast_to(scale[:, lane + 1 : lane + 2], (SUB, LANES))
+            both = jnp.concatenate([above, below], axis=0)
+            spots = slice(i, i + 2 * SUB)
+            for tile in range(tiles):
+                cols = slice(tile * LANES, (tile + 1) * LANES)
+                out_ref[spots, cols] = (y_ref[tile, spots, :] * both).astype(out_ref.dtype)
+        part = pl.ds(n * chunk, chunk)
+        copies.append(pltpu.make_async_copy(out_ref.at[part], out_hbm.at[part], sems.at[n]))
+        copies[-1].start()
+    for copy in copies:
+        copy.wait()
 
 
 def per_device(devices, chans, q, k, v, residues, rates, skip, gain):
@@ -502,14 +517,17 @@
     by_token = vmem((tokens, LANES), F32)
     by_chip = vmem((chips, modes // len(OWNER_Z), LANES), F32)
     packed = vmem((tiles, modes, LANES), F32)
-    return pl.pallas_call(
+    y, scale = pl.pallas_call(
         functools.partial(body, float(tokens * devices)),
-        out_shape=jax.ShapeDtypeStruct((tokens, channels), bf16),
+        out_shape=[
+            jax.ShapeDtypeStruct((tiles, tokens, LANES), F32),
+            jax.ShapeDtypeStruct((SUB, LANES), F32),
+        ],
         in_specs=[pl.BlockSpec(memory_space=pltpu.HBM)] * len(inputs),
-        out_specs=pl.BlockSpec(memory_space=vmem),
+        out_specs=[pl.BlockSpec(memory_space=vmem)] * 2,
         scratch_shapes=[whole, whole, whole, table, table, line, line]
         + [vmem((len(POWERS), tiles, modes, LANES), F32)]
-        + [by_token, by_token, by_tile, by_tile, by_mode, by_mode]
+        + [by_token, by_token, by_tile, by_mode, by_mode]
         + [packed, packed, packed, packed, vmem((modes, LANES), F32), by_token]
         + [by_chip, by_chip]
         + [vmem((SUB, LANES), F32), vmem((chans - 1, SUB, LANES), F32)]
@@ -519,6 +537,14 @@
             collective_id=0, has_side_effects=True, vmem_limit_bytes=24 * 1024 * 1024
         ),
     )(*[pltpu.with_memory_space_constraint(a, pltpu.HBM) for a in inputs])
+    return pl.pallas_call(
+        finish,
+        out_shape=jax.ShapeDtypeStruct((tokens, channels), bf16),
+        in_specs=[pl.BlockSpec(memory_space=vmem)] * 2,
+        out_specs=pl.BlockSpec(memory_space=pltpu.HBM),
+        scratch_shapes=[whole, dma((4,))],
+        compiler_params=pltpu.CompilerParams(vmem_limit_bytes=16 * 1024 * 1024),
+    )(*[pltpu.with_memory_space_constraint(a, pltpu.VMEM) for a in (y, scale)])
 
 
 def solution(mesh):

time: 23.5 us -> 23.5 us (level)
  local copies, waits for them, and re-layouts: 0.8 us -> 0 us
  Pallas kernels: 22.6 us -> 23.3 us
    pallas_call x0 -> x1, Pallas kernels: none -> 0.91 us  [per_device(): pl.pallas_call(finish, out_shape=jax.ShapeDtypeStruct((tokens, channels),...]
    unnamed x1 -> x0, local copies, waits for them, and re-layouts: 0.8 us -> none
where the time goes in v6:
time: 23.5 us; the launch traced here: 23.4 us
  Pallas kernels  23.3 us (99%)
    pallas_call x1, Pallas kernels, per_device(): pl.pallas_call(functools.partial(body, float(tokens * devices)), out_shap...  22.4 us
    pallas_call x1, Pallas kernels, per_device(): pl.pallas_call(finish, out_shape=jax.ShapeDtypeStruct((tokens, channels),...  0.91 us

profile of v6, /device:TPU:6, one launch (start us, length us, event | category | flops | bytes accessed | tf_op | source)
XLA Modules:
  0.0 23.4 jit_solution(11067343445637264327)
XLA Ops:
  0.0 22.4 %shard_map.73 = (f32[8,256,128]{2,1,0:T(8,128)S(1)}, f32[8,128]{1,0:T(8,128)S(1)}) custom-call(bf16[256,1024]{1,0:T(8,128)(2,1)} %q_hbm.1, bf16[256,1024]{1,0:T(8,128)(2,1)} %k_hbm.1, bf16[256,1024]{1,0:T(8,128)(2,1)} %v_hbm.1, f32[16,1024]{1,0:T(8,128)} %bitcast.4, f32[16,1024]{1,0:T(8,128)} %bitcast.5, f32[1,1024]{1,0:T(1,128)} %bitcast.6, f32[1,1024]{1,0:T(1,128)} %bitcast.7), custom_call_target="tpu_custom_call" | custom-call | tf_op jit(solution)/shard_map/pallas_call | solution.py:520
  22.4 0.9 %shard_map.74 = bf16[256,1024]{1,0:T(8,128)(2,1)} custom-call(f32[8,256,128]{2,1,0:T(8,128)S(1)} %get-tuple-element.7.y_ref, f32[8,128]{1,0:T(8,128)S(1)} %get-tuple-element.8.scale_ref), custom_call_target="tpu_custom_call" | custom-call | tf_op jit(solution)/shard_map/pallas_call | solution.py:540
